TPU v7x, 32 devices: a whole 2x2x4 slice. The times are simulated.
32 devices in a mesh: inner: 16 (over z, y, x), outer: 2 (over core).
Axes of the slice: x: 2, y: 2, z: 4, core: 2. Of those that a mesh axis runs over, the one named last changes fastest.
Arguments:
- feats_first: bfloat16 [2, 4096, 2048], P('outer', 'inner'), may hold values from -4 to 8
- feats_second: bfloat16 [2, 4096, 2048], P('outer', 'inner'), may hold values from -4 to 8
- expander: bfloat16 [2048, 1024], P('inner'), may hold values from -0.125 to 0.125
- tile_count: int32 [2, 16], replicated, may hold values from 64 to 256, as said below
- match_dev: int32 [2, 4096, 1], P('outer', 'inner'), may hold values from 0 to 15; in each aligned block of 256 rows (0 to 255, 256 to 511, ..., all dimensions but the last counted through in order) at most 48 rows name the same one
- match_tile: int32 [2, 4096], P('outer', 'inner'), may hold values from 0 to 255
Outputs:
- covariance: float32 [1024, 1024], P('inner')
- invariance: float32 [2, 4096], P('outer', 'inner')
Inputs may be any that keep to these rules, and one draw needn't show every extreme that they name: `tile_count`: for every slide some device has all 256 tiles live; the others at least a quarter. `match_dev`: at most 48 tiles of one device name the same device.
All inputs are finite; a program needn't handle non-finite values.
Results may differ from a plain program's by a relative error of at most 0.00135.
Values may be sent and summed in bfloat16 or wider, within the bound.
A program may use at most 64 MiB of HBM per device.

v0:
```python
import jax
import jax.numpy as jnp
from jax import lax
from jax.sharding import PartitionSpec as P


def shards(feats_first, feats_second, expander, tile_count, match_dev, match_tile):
    first_rows = feats_first[0]
    second_rows = feats_second[0]
    tile_rows = first_rows.shape[0]
    expand_width = expander.shape[1]
    group_size = lax.axis_size("inner")
    capacity = -(-max(2, 3 * tile_rows // group_size) // 16) * 16
    slots = group_size * capacity
    inner_pos = lax.axis_index("inner")
    outer_pos = lax.axis_index("outer")
    target_dev = match_dev[0, :, 0]
    target_tile = match_tile[0]
    row_index = jnp.arange(tile_rows, dtype=jnp.int32)
    same = (target_dev[:, None] == target_dev[None, :]) & (row_index[None, :] < row_index[:, None])
    slot_pos = jnp.sum(same.astype(jnp.int32), axis=1)
    slot = target_dev * capacity + slot_pos
    chosen = slot[:, None] == jnp.arange(slots, dtype=jnp.int32)[None, :]
    asked = jnp.sum(jnp.where(chosen, target_tile[:, None], 0), axis=0).reshape(
        group_size, capacity
    )
    wanted = lax.all_to_all(asked, "inner", split_axis=0, concat_axis=0, tiled=True).reshape(slots)
    piece = lax.all_gather(expander, "inner", axis=0, tiled=True)
    first_embed = jnp.dot(first_rows, piece, preferred_element_type=jnp.float32).astype(
        jnp.bfloat16
    )
    second_embed = jnp.dot(second_rows, piece, preferred_element_type=jnp.float32).astype(
        jnp.bfloat16
    )
    pick = (wanted[:, None] == row_index[None, :]).astype(jnp.bfloat16)
    send_rows = jnp.dot(pick, second_embed, preferred_element_type=jnp.float32).astype(jnp.bfloat16)
    recv_rows = lax.all_to_all(
        send_rows.reshape(group_size, capacity, expand_width),
        "inner",
        split_axis=0,
        concat_axis=0,
        tiled=True,
    ).reshape(slots, expand_width)
    partner = jnp.dot(chosen.astype(jnp.bfloat16), recv_rows, preferred_element_type=jnp.float32)
    counts = lax.dynamic_index_in_dim(tile_count, outer_pos, 0, keepdims=False)
    own_count = lax.dynamic_index_in_dim(counts, inner_pos, 0, keepdims=False)
    live = row_index < own_count
    dest_count = jnp.sum(
        jnp.where(
            target_dev[:, None] == jnp.arange(group_size, dtype=jnp.int32)[None, :],
            counts[None, :],
            0,
        ),
        axis=1,
    )
    valid = live & (target_tile < dest_count)
    diff = first_embed.astype(jnp.float32) - partner
    invariance = jnp.where(valid, jnp.mean(diff * diff, axis=-1), jnp.float32(0.0))
    masked = jnp.where(live[:, None], first_embed, jnp.zeros_like(first_embed))
    column_total = lax.psum(jnp.sum(masked.astype(jnp.float32), axis=0), ("inner", "outer"))
    total = jnp.sum(tile_count).astype(jnp.float32)
    share_rows = expand_width // group_size
    local_share = lax.psum_scatter(
        lax.dot_general(
            masked, masked, (((0,), (0,)), ((), ())), preferred_element_type=jnp.float32
        ),
        "inner",
        scatter_dimension=0,
        tiled=True,
    )
    gram_share = lax.psum(local_share, "outer")
    own_sums = lax.dynamic_slice_in_dim(column_total, inner_pos * share_rows, share_rows, 0)
    covariance = (gram_share - own_sums[:, None] * column_total[None, :] / total) / (total - 1.0)
    return (covariance, invariance[None, :])


def solution(mesh):
    return jax.shard_map(
        shards,
        mesh=mesh,
        in_specs=(
            P("outer", "inner", None),
            P("outer", "inner", None),
            P("inner", None),
            P(),
            P("outer", "inner", None),
            P("outer", "inner"),
        ),
        out_specs=(P("inner", None), P("outer", "inner")),
        check_vma=False,
    )
```

profile of v0, /device:TPU:0, one launch (start us, length us, event | category | flops | bytes accessed | tf_op | source)
XLA Modules:
  0.0 239.3 jit_solution(4994649485600865249)
XLA Ops:
  7.2 0.0 copy-start
  7.2 0.0 all-gather.2.cloned.1.call-start
  7.2 0.7 all-gather.2.cloned.1.call-update
  7.9 0.0 reduce-scatter.2.cloned.1.call-start
  8.0 1.3 dynamic_slice.11
  9.2 0.6 iota_compare_fusion.6
  9.9 79.7 %all-gather.2.cloned.1.call-done = bf16[2048,1024]{1,0:T(8,128)(2,1)} async-done(((bf16[128,1024]{1,0:T(8,128)(2,1)}), bf16[2048,1024]{1,0:T(8,128)(2,1)}) %all-gather.2.cloned.1.call-update) | async-done | bytes 4194320 | tf_op jit(solution)/shard_map/all_gather | solution.py:28
  89.6 3.8 %convert_reduce_fusion = (f32[1024]{0:T(1024)S(1)}, bf16[256,1024]{1,0:T(8,128)(2,1)S(1)}) fusion(pred[256]{0:T(512)(128)(4,1)S(1)} %iota_compare_fusion.6, bf16[2048,1024]{1,0:T(8,128)(2,1)} %all-gather.2.cloned.1.call-done, bf16[1,256,2048]{2,1,0:T(8,128)(2,1)} %param.6), kind=kOutput, calls=%fused_computation.8 | convolution fusion | flops 1074789376 | bytes 5771520 | tf_op jit(solution)/shard_map/dot_general | solution.py:29
  93.4 0.0 copy-start.1
  93.4 0.0 copy-start.2
  93.4 2.8 %fusion.8 = f32[1024,1024]{1,0:T(8,128)} fusion(bf16[256,1024]{1,0:T(8,128)(2,1)S(1)} %get-tuple-element.3, pred[256]{0:T(512)(128)(4,1)S(1)} %iota_compare_fusion.6), kind=kOutput, calls=%fused_computation.19 | convolution fusion | flops 537133056 | bytes 4718848 | tf_op jit(solution)/shard_map/dot_general | solution.py:64
  96.2 0.0 reduce-scatter.2.cloned.1.call-update
  96.2 0.0 copy-done.1
  96.2 0.2 convert_reduce_fusion.1
  96.4 0.0 copy-done.2
  96.4 0.2 select_reduce_fusion
  96.6 0.1 all_to_all.9
  96.7 11.4 %all_to_all.14 = s32[16,1,48]{2,1,0:T(1,128)S(1)} all-to-all(s32[16,1,48]{2,1,0:T(1,128)S(1)} %all_to_all.9), channel_id=1, replica_groups=mesh['inner'=16,'outer'=2] {'inner'}, dimensions={0} | all-to-all | bytes 6144 | tf_op jit(solution)/shard_map/all_to_all | solution.py:27
  108.0 0.5 broadcast.32
  108.5 0.7 reduce.3
  109.2 0.1 eq.66
  109.3 0.0 copy-done
  109.3 0.0 copy-start.3
  109.3 5.1 %convolution_convert_fusion = bf16[768,1024]{1,0:T(8,128)(2,1)} fusion(bf16[2048,1024]{1,0:T(8,128)(2,1)} %all-gather.2.cloned.1.call-done, bf16[1,256,2048]{2,1,0:T(8,128)(2,1)S(1)} %copy-done, s32[768]{0:T(1024)S(1)} %eq.66), kind=kOutput, calls=%fused_computation | convolution fusion | flops 1477640192 | bytes 6818816 | tf_op jit(solution)/shard_map/dot_general | solution.py:36
  114.4 3.8 %all-to-all-start.1 = ((bf16[16,48,1024]{2,1,0:T(8,128)(2,1)}), bf16[16,48,1024]{2,1,0:T(8,128)(2,1)S(1)}, u32[]{:S(2)}, u32[]{:S(2)}) async-start(bf16[16,48,1024]{2,1,0:T(8,128)(2,1)} %bitcast.22), calls=%async_computation.2 | async-start | bytes 3145728 | tf_op jit(solution)/shard_map/all_to_all | solution.py:37
  118.2 0.0 all-reduce.2.cloned.1.call-start
  118.3 0.0 copy-done.3
  118.3 0.6 reduce_sum.57
  119.6 0.1 select_reduce_fusion.1
  119.7 71.8 %psum.15 = f32[1024]{0:T(1024)S(1)} all-reduce(f32[1024]{0:T(1024)S(1)} %get-tuple-element.2), channel_id=1, replica_groups=mesh['inner'=16,'outer'=2] {'inner','outer'}, use_global_device_ids=true, to_apply=%region_3.4 | all-reduce | flops 1024 | bytes 8192 | tf_op jit(solution)/shard_map/psum | solution.py:60
  191.4 0.1 dynamic_slice.12
  191.5 0.0 all-to-all-done.1
  191.5 0.7 fusion.1
  192.3 19.4 %reduce-scatter.2.cloned.1.call-done = f32[64,1024]{1,0:T(8,128)} async-done(((f32[1024,1024]{1,0:T(8,128)}), f32[64,1024]{1,0:T(8,128)}) %reduce-scatter.2.cloned.1.call-update) | async-done | bytes 262160 | tf_op jit(solution)/shard_map/reduce_scatter | solution.py:63
  211.7 0.0 all-reduce.2.cloned.1.call-update
  211.7 1.2 and_select_fusion
  212.9 18.0 %all-reduce.2.cloned.1.call-done = f32[64,1024]{1,0:T(8,128)} async-done(((f32[64,1024]{1,0:T(8,128)}), f32[64,1024]{1,0:T(8,128)}) %all-reduce.2.cloned.1.call-update) | async-done | bytes 262160 | tf_op jit(solution)/shard_map/psum | solution.py:71
  231.0 1.8 subtract_divide_fusion
  (3 shorter events, 0.0 us)
Async XLA Ops:
  7.2 102.1 %copy-start = (bf16[1,256,2048]{2,1,0:T(8,128)(2,1)S(1)}, bf16[1,256,2048]{2,1,0:T(8,128)(2,1)}, u32[]{:S(2)}) copy-start(bf16[1,256,2048]{2,1,0:T(8,128)(2,1)} %param.7) | copy-start | bytes 3145732
  7.2 82.4 %all-gather.2.cloned.1.call-start = ((), (), s32[]{:S(2)}) async-start(), calls=%async_computation.3 | async-start | bytes 4456448 | tf_op jit(solution)/shard_map/all_gather | solution.py:28
  7.9 203.8 %reduce-scatter.2.cloned.1.call-start = ((), (), s32[]{:S(2)}) async-start(), calls=%async_computation.4 | async-start | bytes 4456448 | tf_op jit(solution)/shard_map/reduce_scatter | solution.py:63
  93.4 2.8 %copy-start.1 = (s32[1,256,1]{1,2,0:T(1,128)S(1)}, s32[1,256,1]{1,2,0:T(1,128)}, u32[]{:S(2)}) copy-start(s32[1,256,1]{1,2,0:T(1,128)} %param.10) | copy-start | bytes 3076
  93.4 3.0 %copy-start.2 = (s32[1,256]{1,0:T(1,128)S(1)}, s32[1,256]{1,0:T(1,128)}, u32[]{:S(2)}) copy-start(s32[1,256]{1,0:T(1,128)} %param.11) | copy-start | bytes 3076
  109.3 9.0 %copy-start.3 = (s32[2,16]{1,0:T(2,128)S(1)}, s32[2,16]{1,0:T(2,128)}, u32[]{:S(2)}) copy-start(s32[2,16]{1,0:T(2,128)} %param.9) | copy-start | bytes 388
  114.4 77.1 %all-to-all-start.1 = ((bf16[16,48,1024]{2,1,0:T(8,128)(2,1)}), bf16[16,48,1024]{2,1,0:T(8,128)(2,1)S(1)}, u32[]{:S(2)}, u32[]{:S(2)}) async-start(bf16[16,48,1024]{2,1,0:T(8,128)(2,1)} %bitcast.22), calls=%async_computation.2 | async-start | bytes 3145728 | tf_op jit(solution)/shard_map/all_to_all | solution.py:37
  118.2 112.8 %all-reduce.2.cloned.1.call-start = ((), (), s32[]{:S(2)}) async-start(), calls=%async_computation.5 | async-start | bytes 524288 | tf_op jit(solution)/shard_map/psum | solution.py:71
Sparse Core Ops, SparseCore 0:
  10.8 78.7 all-gather.1
  96.3 115.3 reduce-scatter.1
  214.0 16.9 all-reduce.1
where the time goes:
time: 240 us; the launch traced here: 239 us
  waiting for transfers between devices  118 us (49%)
  blocking collectives  83.1 us (35%)
  between operations  14.5 us (6%)
  matrix products  12.4 us (5%)
  other arithmetic  5.35 us (2%)
  starting transfers between devices  3.88 us (2%)
    all_gather x1, waiting for transfers between devices, shards(): piece = lax.all_gather(expander, 'inner', axis=0, tiled=True)  79.7 us
    psum x1, blocking collectives, shards(): lax.psum(jnp.sum(masked.astype(jnp.float32), axis=0), ('inner', 'outer'))  71.8 us
    reduce_scatter x1, waiting for transfers between devices, shards(): lax.psum_scatter(lax.dot_general(masked, masked, (((0,), (0,)), ((), ()))...  19.4 us
    psum x1, waiting for transfers between devices, shards(): gram_share = lax.psum(local_share, 'outer')  18 us
    all_to_all x1, blocking collectives, shards(): lax.all_to_all(asked, 'inner', split_axis=0, concat_axis=0, tiled=True)  11.4 us
    dot_general x1, matrix products, shards(): jnp.dot(pick, second_embed, preferred_element_type=jnp.float32)  5.14 us
  transfers between devices with their start and end apart: 4, of which 3 were waited for; matrix products, arithmetic and copies ran while one was open for 5% of the time, Pallas kernels for 0%

commit v1 on v0

--- a/solution.py
+++ b/solution.py
@@ -2,6 +2,29 @@
 import jax.numpy as jnp
 from jax import lax
 from jax.sharding import PartitionSpec as P
+
+
+def in_blocks(x, dim, size):
+    before, after = (x.shape[:dim], x.shape[dim + 1 :])
+    return jnp.moveaxis(x.reshape(*before, size, -1, *after), dim, 0)
+
+
+def in_order(blocks, dim):
+    blocks = jnp.moveaxis(blocks, 0, dim)
+    shape = blocks.shape
+    return blocks.reshape(*shape[:dim], shape[dim] * shape[dim + 1], *shape[dim + 2 :])
+
+
+def sent_to_each(array, axis, split_dim, concat_dim):
+    size, mine = (lax.axis_size(axis), lax.axis_index(axis))
+    blocks = in_blocks(array, split_dim, size)
+    out = blocks
+    for step in range(1, size):
+        target, source = ((mine + step) % size, (mine - step) % size)
+        sent = lax.dynamic_index_in_dim(blocks, target, 0)
+        theirs = lax.ppermute(sent, axis, [(i, (i + step) % size) for i in range(size)])
+        out = lax.dynamic_update_slice_in_dim(out, theirs, source, axis=0)
+    return in_order(out, concat_dim)
 
 
 def shards(feats_first, feats_second, expander, tile_count, match_dev, match_tile):
@@ -24,7 +47,7 @@
     asked = jnp.sum(jnp.where(chosen, target_tile[:, None], 0), axis=0).reshape(
         group_size, capacity
     )
-    wanted = lax.all_to_all(asked, "inner", split_axis=0, concat_axis=0, tiled=True).reshape(slots)
+    wanted = sent_to_each(asked, "inner", 0, 0).reshape(slots)
     piece = lax.all_gather(expander, "inner", axis=0, tiled=True)
     first_embed = jnp.dot(first_rows, piece, preferred_element_type=jnp.float32).astype(
         jnp.bfloat16

time: 240 us -> 257 us (1.071)
  blocking collectives: 83.1 us -> 56 us
  waiting for transfers between devices: 118 us -> 142 us
  starting transfers between devices: 3.88 us -> 24.3 us
    ppermute x0 -> x15, waiting for transfers between devices: none -> 44.7 us  [sent_to_each(): lax.ppermute(sent, axis, [(i, (i + step) % size) for i in range(size)])]
    reduce_scatter x1, waiting for transfers between devices: 19.4 us -> 0.02 us  [shards(): lax.psum_scatter(lax.dot_general(masked, masked, (((0,), (0,)), ((), ()))...]
    ppermute x0 -> x15, starting transfers between devices: none -> 17 us  [sent_to_each(): lax.ppermute(sent, axis, [(i, (i + step) % size) for i in range(size)])]
    psum x1, blocking collectives: 71.8 us -> 56 us  [shards(): lax.psum(jnp.sum(masked.astype(jnp.float32), axis=0), ('inner', 'outer'))]
    all_to_all x1 -> x0, blocking collectives: 11.4 us -> none  [shards(): lax.all_to_all(asked, 'inner', split_axis=0, concat_axis=0, tiled=True)]
    all_to_all x1, starting transfers between devices: 3.76 us -> 7.14 us  [shards(): lax.all_to_all(send_rows.reshape(group_size, capacity, expand_width), 'in...]
  transfers between devices with their start and end apart: 4 -> 19, of which waited for: 3 -> 13; matrix products, arithmetic and copies ran while one was open for 5% -> 5% of each run, Pallas kernels for 0% -> 0%
where the time goes in v1:
time: 257 us
  waiting for transfers between devices  142 us (55%)
  blocking collectives  56 us (22%)
  starting transfers between devices  24.3 us (9%)
  between operations  14.6 us (6%)
  matrix products  12.4 us (5%)
  other arithmetic  5.35 us (2%)
    all_gather x1, waiting for transfers between devices, shards(): piece = lax.all_gather(expander, 'inner', axis=0, tiled=True)  79.7 us
    psum x1, blocking collectives, shards(): lax.psum(jnp.sum(masked.astype(jnp.float32), axis=0), ('inner', 'outer'))  56 us
    ppermute x15, waiting for transfers between devices, sent_to_each(): lax.ppermute(sent, axis, [(i, (i + step) % size) for i in range(size)])  44.7 us
    ppermute x15, starting transfers between devices, sent_to_each(): lax.ppermute(sent, axis, [(i, (i + step) % size) for i in range(size)])  17 us
    psum x1, waiting for transfers between devices, shards(): gram_share = lax.psum(local_share, 'outer')  16.9 us
    all_to_all x1, starting transfers between devices, shards(): lax.all_to_all(send_rows.reshape(group_size, capacity, expand_width), 'in...  7.14 us
  transfers between devices with their start and end apart: 19, of which 13 were waited for; matrix products, arithmetic and copies ran while one was open for 5% of the time, Pallas kernels for 0%

profile of v1, /device:TPU:0, one launch (start us, length us, event | category | flops | bytes accessed | tf_op | source)
XLA Modules:
  0.0 257.0 jit_solution(1716849974062889088)
XLA Ops:
  7.2 0.0 copy-start
  7.2 0.0 all-gather.2.cloned.1.call-start
  7.2 0.7 all-gather.2.cloned.1.call-update
  7.9 0.0 reduce-scatter.2.cloned.1.call-start
  8.0 1.3 dynamic_slice.57
  9.2 0.6 iota_compare_fusion.6
  9.9 79.7 %all-gather.2.cloned.1.call-done = bf16[2048,1024]{1,0:T(8,128)(2,1)} async-done(((bf16[128,1024]{1,0:T(8,128)(2,1)}), bf16[2048,1024]{1,0:T(8,128)(2,1)}) %all-gather.2.cloned.1.call-update) | async-done | bytes 4194320 | tf_op jit(solution)/shard_map/all_gather | solution.py:51
  89.6 3.8 %convert_reduce_fusion = (f32[1024]{0:T(1024)S(1)}, bf16[256,1024]{1,0:T(8,128)(2,1)S(1)}) fusion(pred[256]{0:T(512)(128)(4,1)S(1)} %iota_compare_fusion.6, bf16[2048,1024]{1,0:T(8,128)(2,1)} %all-gather.2.cloned.1.call-done, bf16[1,256,2048]{2,1,0:T(8,128)(2,1)} %param.6), kind=kOutput, calls=%fused_computation.8 | convolution fusion | flops 1074789376 | bytes 5771520 | tf_op jit(solution)/shard_map/dot_general | solution.py:52
  93.4 0.0 copy-start.1
  93.4 0.0 copy-start.2
  93.4 2.8 %fusion.8 = f32[1024,1024]{1,0:T(8,128)} fusion(bf16[256,1024]{1,0:T(8,128)(2,1)S(1)} %get-tuple-element.18, pred[256]{0:T(512)(128)(4,1)S(1)} %iota_compare_fusion.6), kind=kOutput, calls=%fused_computation.19 | convolution fusion | flops 537133056 | bytes 4718848 | tf_op jit(solution)/shard_map/dot_general | solution.py:87
  96.2 0.0 reduce-scatter.2.cloned.1.call-update
  96.2 0.0 copy-done.1
  96.2 0.2 convert_reduce_fusion.1
  96.4 0.2 select_reduce_fusion
  96.6 0.1 reshape_reshape.3
  96.7 1.5 collective-permute-start
  98.2 5.7 %collective-permute-done = s32[1,1,48]{2,1,0:T(1,128)S(1)} collective-permute-done((s32[1,1,48]{2,1,0:T(1,128)S(1)}, s32[1,1,48]{2,1,0:T(1,128)S(1)}, u32[]{:S(2)}, u32[]{:S(2)}) %collective-permute-start) | collective-permute-done | bytes 224 | tf_op jit(solution)/shard_map/ppermute | solution.py:25
  103.9 0.1 collective-permute-start.14
  104.0 0.6 collective-permute-start.13
  104.6 1.4 collective-permute-start.1
  106.1 1.5 collective-permute-start.12
  107.6 1.5 collective-permute-start.11
  109.1 1.8 collective-permute-done.1
  110.9 0.2 collective-permute-start.2
  111.0 6.1 %collective-permute-done.2 = s32[1,1,48]{2,1,0:T(1,128)S(1)} collective-permute-done((s32[1,1,48]{2,1,0:T(1,128)S(1)}, s32[1,1,48]{2,1,0:T(1,128)S(1)}, u32[]{:S(2)}, u32[]{:S(2)}) %collective-permute-start.2) | collective-permute-done | bytes 224 | tf_op jit(solution)/shard_map/ppermute | solution.py:25
  117.1 0.0 collective-permute-start.3
  117.1 5.3 %collective-permute-done.3 = s32[1,1,48]{2,1,0:T(1,128)S(1)} collective-permute-done((s32[1,1,48]{2,1,0:T(1,128)S(1)}, s32[1,1,48]{2,1,0:T(1,128)S(1)}, u32[]{:S(2)}, u32[]{:S(2)}) %collective-permute-start.3) | collective-permute-done | bytes 224 | tf_op jit(solution)/shard_map/ppermute | solution.py:25
  122.5 0.0 collective-permute-start.4
  122.5 6.3 %collective-permute-done.4 = s32[1,1,48]{2,1,0:T(1,128)S(1)} collective-permute-done((s32[1,1,48]{2,1,0:T(1,128)S(1)}, s32[1,1,48]{2,1,0:T(1,128)S(1)}, u32[]{:S(2)}, u32[]{:S(2)}) %collective-permute-start.4) | collective-permute-done | bytes 224 | tf_op jit(solution)/shard_map/ppermute | solution.py:25
  128.8 0.0 collective-permute-start.5
  128.8 5.4 %collective-permute-done.5 = s32[1,1,48]{2,1,0:T(1,128)S(1)} collective-permute-done((s32[1,1,48]{2,1,0:T(1,128)S(1)}, s32[1,1,48]{2,1,0:T(1,128)S(1)}, u32[]{:S(2)}, u32[]{:S(2)}) %collective-permute-start.5) | collective-permute-done | bytes 224 | tf_op jit(solution)/shard_map/ppermute | solution.py:25
  134.2 0.8 collective-permute-start.6
  135.0 4.5 %collective-permute-done.6 = s32[1,1,48]{2,1,0:T(1,128)S(1)} collective-permute-done((s32[1,1,48]{2,1,0:T(1,128)S(1)}, s32[1,1,48]{2,1,0:T(1,128)S(1)}, u32[]{:S(2)}, u32[]{:S(2)}) %collective-permute-start.6) | collective-permute-done | bytes 224 | tf_op jit(solution)/shard_map/ppermute | solution.py:25
  139.5 0.8 collective-permute-start.7
  140.3 3.7 %collective-permute-done.7 = s32[1,1,48]{2,1,0:T(1,128)S(1)} collective-permute-done((s32[1,1,48]{2,1,0:T(1,128)S(1)}, s32[1,1,48]{2,1,0:T(1,128)S(1)}, u32[]{:S(2)}, u32[]{:S(2)}) %collective-permute-start.7) | collective-permute-done | bytes 224 | tf_op jit(solution)/shard_map/ppermute | solution.py:25
  144.0 2.6 %collective-permute-start.8 = (s32[1,1,48]{2,1,0:T(1,128)S(1)}, s32[1,1,48]{2,1,0:T(1,128)S(1)}, u32[]{:S(2)}, u32[]{:S(2)}) collective-permute-start(s32[1,1,48]{2,1,0:T(1,128)S(1)} %get-tuple-element.8), channel_id=1, source_target_pairs={{0,18},{2,20},{4,22},{6,24},{8,26},{10,28},{12,30},{14,0},{16,2},{... | collective-permute-start | bytes 584 | tf_op jit(solution)/shard_map/ppermute | solution.py:25
  146.6 2.8 %collective-permute-done.8 = s32[1,1,48]{2,1,0:T(1,128)S(1)} collective-permute-done((s32[1,1,48]{2,1,0:T(1,128)S(1)}, s32[1,1,48]{2,1,0:T(1,128)S(1)}, u32[]{:S(2)}, u32[]{:S(2)}) %collective-permute-start.8) | collective-permute-done | bytes 224 | tf_op jit(solution)/shard_map/ppermute | solution.py:25
  149.3 2.6 %collective-permute-start.9 = (s32[1,1,48]{2,1,0:T(1,128)S(1)}, s32[1,1,48]{2,1,0:T(1,128)S(1)}, u32[]{:S(2)}, u32[]{:S(2)}) collective-permute-start(s32[1,1,48]{2,1,0:T(1,128)S(1)} %get-tuple-element.7), channel_id=1, source_target_pairs={{0,20},{2,22},{4,24},{6,26},{8,28},{10,30},{12,0},{14,2},{16,4},{1... | collective-permute-start | bytes 584 | tf_op jit(solution)/shard_map/ppermute | solution.py:25
  151.9 1.9 collective-permute-done.9
  153.8 3.5 %collective-permute-start.10 = (s32[1,1,48]{2,1,0:T(1,128)S(1)}, s32[1,1,48]{2,1,0:T(1,128)S(1)}, u32[]{:S(2)}, u32[]{:S(2)}) collective-permute-start(s32[1,1,48]{2,1,0:T(1,128)S(1)} %get-tuple-element.6), channel_id=1, source_target_pairs={{0,22},{2,24},{4,26},{6,28},{8,30},{10,0},{12,2},{14,4},{16,6},{18... | collective-permute-start | bytes 584 | tf_op jit(solution)/shard_map/ppermute | solution.py:25
  157.2 1.3 collective-permute-done.10
  158.5 0.0 collective-permute-done.11
  158.5 0.0 collective-permute-done.12
  158.6 0.0 collective-permute-done.13
  158.6 0.0 collective-permute-done.14
  158.6 0.5 broadcast.62
  159.1 0.7 reduce.3
  159.8 0.1 eq.97
  159.9 5.1 %convolution_convert_fusion = bf16[768,1024]{1,0:T(8,128)(2,1)} fusion(bf16[2048,1024]{1,0:T(8,128)(2,1)} %all-gather.2.cloned.1.call-done, bf16[1,256,2048]{2,1,0:T(8,128)(2,1)S(1)} %copy-done, s32[768]{0:T(1024)S(1)} %eq.97), kind=kOutput, calls=%fused_computation | convolution fusion | flops 1477640192 | bytes 6818816 | tf_op jit(solution)/shard_map/dot_general | solution.py:59
  165.0 7.1 %all-to-all-start = ((bf16[16,48,1024]{2,1,0:T(8,128)(2,1)}), bf16[16,48,1024]{2,1,0:T(8,128)(2,1)S(1)}, u32[]{:S(2)}, u32[]{:S(2)}) async-start(bf16[16,48,1024]{2,1,0:T(8,128)(2,1)} %bitcast.22), calls=%async_computation.1 | async-start | bytes 3145728 | tf_op jit(solution)/shard_map/all_to_all | solution.py:60
  172.2 0.0 all-reduce.2.cloned.1.call-start
  172.2 0.0 copy-done.3
  172.2 0.6 reduce_sum.57
  173.5 0.1 select_reduce_fusion.1
  173.6 56.0 %psum.15 = f32[1024]{0:T(1024)S(1)} all-reduce(f32[1024]{0:T(1024)S(1)} %get-tuple-element.17), channel_id=1, replica_groups=mesh['inner'=16,'outer'=2] {'inner','outer'}, use_global_device_ids=true, to_apply=%region_3.4 | all-reduce | flops 1024 | bytes 8192 | tf_op jit(solution)/shard_map/psum | solution.py:83
  229.7 0.1 dynamic_slice.58
  229.7 0.0 all-to-all-done
  229.7 0.7 fusion.1
  230.5 0.0 reduce-scatter.2.cloned.1.call-done
  230.5 0.0 all-reduce.2.cloned.1.call-update
  230.5 1.2 and_select_fusion
  231.8 16.9 %all-reduce.2.cloned.1.call-done = f32[64,1024]{1,0:T(8,128)} async-done(((f32[64,1024]{1,0:T(8,128)}), f32[64,1024]{1,0:T(8,128)}) %all-reduce.2.cloned.1.call-update) | async-done | bytes 262160 | tf_op jit(solution)/shard_map/psum | solution.py:94
  248.7 1.8 subtract_divide_fusion
  (22 shorter events, 0.2 us)
Async XLA Ops:
  7.2 152.7 %copy-start = (bf16[1,256,2048]{2,1,0:T(8,128)(2,1)S(1)}, bf16[1,256,2048]{2,1,0:T(8,128)(2,1)}, u32[]{:S(2)}) copy-start(bf16[1,256,2048]{2,1,0:T(8,128)(2,1)} %param.7) | copy-start | bytes 3145732
  7.2 82.4 %all-gather.2.cloned.1.call-start = ((), (), s32[]{:S(2)}) async-start(), calls=%async_computation.2 | async-start | bytes 4456448 | tf_op jit(solution)/shard_map/all_gather | solution.py:51
  7.9 222.6 %reduce-scatter.2.cloned.1.call-start = ((), (), s32[]{:S(2)}) async-start(), calls=%async_computation.3 | async-start | bytes 4456448 | tf_op jit(solution)/shard_map/reduce_scatter | solution.py:86
  93.4 2.9 %copy-start.1 = (s32[1,256,1]{1,2,0:T(1,128)S(1)}, s32[1,256,1]{1,2,0:T(1,128)}, u32[]{:S(2)}) copy-start(s32[1,256,1]{1,2,0:T(1,128)} %param.10) | copy-start | bytes 3076
  93.4 3.0 %copy-start.2 = (s32[1,256]{1,0:T(1,128)S(1)}, s32[1,256]{1,0:T(1,128)}, u32[]{:S(2)}) copy-start(s32[1,256]{1,0:T(1,128)} %param.11) | copy-start | bytes 3076
  96.7 7.2 %collective-permute-start = (s32[1,1,48]{2,1,0:T(1,128)S(1)}, s32[1,1,48]{2,1,0:T(1,128)S(1)}, u32[]{:S(2)}, u32[]{:S(2)}) collective-permute-start(s32[1,1,48]{2,1,0:T(1,128)S(1)} %constant_dynamic-slice_fusion.14), channel_id=1, source_target_pairs={{0,2},{2,4},{4,6},{6,8},{8,10},{10,12},{12,14},{14,16},{16,18},{18... | collective-permute-start | bytes 584 | tf_op jit(solution)/shard_map/ppermute | solution.py:25
  103.9 54.7 %collective-permute-start.14 = (s32[1,1,48]{2,1,0:T(1,128)S(1)}, s32[1,1,48]{2,1,0:T(1,128)S(1)}, u32[]{:S(2)}, u32[]{:S(2)}) collective-permute-start(s32[1,1,48]{2,1,0:T(1,128)S(1)} %get-tuple-element.2), channel_id=1, source_target_pairs={{0,30},{2,0},{4,2},{6,4},{8,6},{10,8},{12,10},{14,12},{16,14},{18,... | collective-permute-start | bytes 584 | tf_op jit(solution)/shard_map/ppermute | solution.py:25
  104.0 54.6 %collective-permute-start.13 = (s32[1,1,48]{2,1,0:T(1,128)S(1)}, s32[1,1,48]{2,1,0:T(1,128)S(1)}, u32[]{:S(2)}, u32[]{:S(2)}) collective-permute-start(s32[1,1,48]{2,1,0:T(1,128)S(1)} %get-tuple-element.3), channel_id=1, source_target_pairs={{0,28},{2,30},{4,0},{6,2},{8,4},{10,6},{12,8},{14,10},{16,12},{18,... | collective-permute-start | bytes 584 | tf_op jit(solution)/shard_map/ppermute | solution.py:25
  104.6 6.2 %collective-permute-start.1 = (s32[1,1,48]{2,1,0:T(1,128)S(1)}, s32[1,1,48]{2,1,0:T(1,128)S(1)}, u32[]{:S(2)}, u32[]{:S(2)}) collective-permute-start(s32[1,1,48]{2,1,0:T(1,128)S(1)} %get-tuple-element.15), channel_id=1, source_target_pairs={{0,4},{2,6},{4,8},{6,10},{8,12},{10,14},{12,16},{14,18},{16,20},{1... | collective-permute-start | bytes 584 | tf_op jit(solution)/shard_map/ppermute | solution.py:25
  106.1 52.5 %collective-permute-start.12 = (s32[1,1,48]{2,1,0:T(1,128)S(1)}, s32[1,1,48]{2,1,0:T(1,128)S(1)}, u32[]{:S(2)}, u32[]{:S(2)}) collective-permute-start(s32[1,1,48]{2,1,0:T(1,128)S(1)} %get-tuple-element.4), channel_id=1, source_target_pairs={{0,26},{2,28},{4,30},{6,0},{8,2},{10,4},{12,6},{14,8},{16,10},{18,... | collective-permute-start | bytes 584 | tf_op jit(solution)/shard_map/ppermute | solution.py:25
  107.6 51.0 %collective-permute-start.11 = (s32[1,1,48]{2,1,0:T(1,128)S(1)}, s32[1,1,48]{2,1,0:T(1,128)S(1)}, u32[]{:S(2)}, u32[]{:S(2)}) collective-permute-start(s32[1,1,48]{2,1,0:T(1,128)S(1)} %get-tuple-element.5), channel_id=1, source_target_pairs={{0,24},{2,26},{4,28},{6,30},{8,0},{10,2},{12,4},{14,6},{16,8},{18,... | collective-permute-start | bytes 584 | tf_op jit(solution)/shard_map/ppermute | solution.py:25
  110.9 6.2 %collective-permute-start.2 = (s32[1,1,48]{2,1,0:T(1,128)S(1)}, s32[1,1,48]{2,1,0:T(1,128)S(1)}, u32[]{:S(2)}, u32[]{:S(2)}) collective-permute-start(s32[1,1,48]{2,1,0:T(1,128)S(1)} %get-tuple-element.14), channel_id=1, source_target_pairs={{0,6},{2,8},{4,10},{6,12},{8,14},{10,16},{12,18},{14,20},{16,22},{... | collective-permute-start | bytes 584 | tf_op jit(solution)/shard_map/ppermute | solution.py:25
  117.1 5.3 %collective-permute-start.3 = (s32[1,1,48]{2,1,0:T(1,128)S(1)}, s32[1,1,48]{2,1,0:T(1,128)S(1)}, u32[]{:S(2)}, u32[]{:S(2)}) collective-permute-start(s32[1,1,48]{2,1,0:T(1,128)S(1)} %get-tuple-element.13), channel_id=1, source_target_pairs={{0,8},{2,10},{4,12},{6,14},{8,16},{10,18},{12,20},{14,22},{16,24},... | collective-permute-start | bytes 584 | tf_op jit(solution)/shard_map/ppermute | solution.py:25
  122.5 6.4 %collective-permute-start.4 = (s32[1,1,48]{2,1,0:T(1,128)S(1)}, s32[1,1,48]{2,1,0:T(1,128)S(1)}, u32[]{:S(2)}, u32[]{:S(2)}) collective-permute-start(s32[1,1,48]{2,1,0:T(1,128)S(1)} %get-tuple-element.12), channel_id=1, source_target_pairs={{0,10},{2,12},{4,14},{6,16},{8,18},{10,20},{12,22},{14,24},{16,26}... | collective-permute-start | bytes 584 | tf_op jit(solution)/shard_map/ppermute | solution.py:25
  128.8 5.4 %collective-permute-start.5 = (s32[1,1,48]{2,1,0:T(1,128)S(1)}, s32[1,1,48]{2,1,0:T(1,128)S(1)}, u32[]{:S(2)}, u32[]{:S(2)}) collective-permute-start(s32[1,1,48]{2,1,0:T(1,128)S(1)} %get-tuple-element.11), channel_id=1, source_target_pairs={{0,12},{2,14},{4,16},{6,18},{8,20},{10,22},{12,24},{14,26},{16,28}... | collective-permute-start | bytes 584 | tf_op jit(solution)/shard_map/ppermute | solution.py:25
  134.2 5.3 %collective-permute-start.6 = (s32[1,1,48]{2,1,0:T(1,128)S(1)}, s32[1,1,48]{2,1,0:T(1,128)S(1)}, u32[]{:S(2)}, u32[]{:S(2)}) collective-permute-start(s32[1,1,48]{2,1,0:T(1,128)S(1)} %get-tuple-element.10), channel_id=1, source_target_pairs={{0,14},{2,16},{4,18},{6,20},{8,22},{10,24},{12,26},{14,28},{16,30}... | collective-permute-start | bytes 584 | tf_op jit(solution)/shard_map/ppermute | solution.py:25
  139.5 4.4 %collective-permute-start.7 = (s32[1,1,48]{2,1,0:T(1,128)S(1)}, s32[1,1,48]{2,1,0:T(1,128)S(1)}, u32[]{:S(2)}, u32[]{:S(2)}) collective-permute-start(s32[1,1,48]{2,1,0:T(1,128)S(1)} %get-tuple-element.9), channel_id=1, source_target_pairs={{0,16},{2,18},{4,20},{6,22},{8,24},{10,26},{12,28},{14,30},{16,0},... | collective-permute-start | bytes 584 | tf_op jit(solution)/shard_map/ppermute | solution.py:25
  144.0 5.3 %collective-permute-start.8 = (s32[1,1,48]{2,1,0:T(1,128)S(1)}, s32[1,1,48]{2,1,0:T(1,128)S(1)}, u32[]{:S(2)}, u32[]{:S(2)}) collective-permute-start(s32[1,1,48]{2,1,0:T(1,128)S(1)} %get-tuple-element.8), channel_id=1, source_target_pairs={{0,18},{2,20},{4,22},{6,24},{8,26},{10,28},{12,30},{14,0},{16,2},{... | collective-permute-start | bytes 584 | tf_op jit(solution)/shard_map/ppermute | solution.py:25
  149.3 4.4 %collective-permute-start.9 = (s32[1,1,48]{2,1,0:T(1,128)S(1)}, s32[1,1,48]{2,1,0:T(1,128)S(1)}, u32[]{:S(2)}, u32[]{:S(2)}) collective-permute-start(s32[1,1,48]{2,1,0:T(1,128)S(1)} %get-tuple-element.7), channel_id=1, source_target_pairs={{0,20},{2,22},{4,24},{6,26},{8,28},{10,30},{12,0},{14,2},{16,4},{1... | collective-permute-start | bytes 584 | tf_op jit(solution)/shard_map/ppermute | solution.py:25
  153.8 4.8 %collective-permute-start.10 = (s32[1,1,48]{2,1,0:T(1,128)S(1)}, s32[1,1,48]{2,1,0:T(1,128)S(1)}, u32[]{:S(2)}, u32[]{:S(2)}) collective-permute-start(s32[1,1,48]{2,1,0:T(1,128)S(1)} %get-tuple-element.6), channel_id=1, source_target_pairs={{0,22},{2,24},{4,26},{6,28},{8,30},{10,0},{12,2},{14,4},{16,6},{18... | collective-permute-start | bytes 584 | tf_op jit(solution)/shard_map/ppermute | solution.py:25
  159.9 12.3 %copy-start.3 = (s32[2,16]{1,0:T(2,128)S(1)}, s32[2,16]{1,0:T(2,128)}, u32[]{:S(2)}) copy-start(s32[2,16]{1,0:T(2,128)} %param.9) | copy-start | bytes 388
  165.0 64.7 %all-to-all-start = ((bf16[16,48,1024]{2,1,0:T(8,128)(2,1)}), bf16[16,48,1024]{2,1,0:T(8,128)(2,1)S(1)}, u32[]{:S(2)}, u32[]{:S(2)}) async-start(bf16[16,48,1024]{2,1,0:T(8,128)(2,1)} %bitcast.22), calls=%async_computation.1 | async-start | bytes 3145728 | tf_op jit(solution)/shard_map/all_to_all | solution.py:60
  172.2 76.5 %all-reduce.2.cloned.1.call-start = ((), (), s32[]{:S(2)}) async-start(), calls=%async_computation.4 | async-start | bytes 524288 | tf_op jit(solution)/shard_map/psum | solution.py:94
Sparse Core Ops, SparseCore 0:
  10.8 78.7 all-gather.1
  96.3 112.4 reduce-scatter.1
  230.6 17.9 all-reduce.1
